TPU v7x, 128 devices: a whole 4x4x4 slice. The times are simulated.
128 devices in a mesh: segment: 2 (over core), fsdp: 32 (over x, y_lo, z), dp: 2 (over y_hi).
Axes of the slice: x: 4, y: 4 (y_hi: 2, y_lo: 2; y = y_hi * 2 + y_lo), z: 4, core: 2. Of those that a mesh axis runs over, the one named last changes fastest.
Arguments:
- hooks: bfloat16 [2, 4, 256, 64, 6144], P('segment', 'dp', 'fsdp'), may hold values from -6 to 6
- proj_weight: bfloat16 [2, 6144, 256], P('segment', 'fsdp'), may hold values from -0.078125 to 0.078125
- conv_weight: bfloat16 [2, 2, 2304, 256], P('segment', None, 'fsdp'), may hold values from -0.125 to 0.125
- head_weight: bfloat16 [3, 256], replicated, may hold values from -0.375 to 0.375
- light_color: float32 [25, 3], replicated, may hold values from 0.3 to 1.5
- illum: int32 [4, 4], P('dp'), may hold values from 0 to 24
- offsets: int32 [4, 4, 2], P('dp'), may hold values from 0 to 32
- photos: bfloat16 [4, 4, 3, 96, 96], P('dp'), may hold values from 0 to 10
Outputs:
- grad_proj: float32 [2, 6144, 256], P('segment', 'fsdp')
- grad_conv: float32 [2, 2, 2304, 256], P('segment', None, 'fsdp')
- grad_head: float32 [3, 256], replicated
- loss: float32 [], replicated
All inputs are finite; a program needn't handle non-finite values.
Results may differ from a plain program's by a relative error of at most 0.018.
Values may be sent and summed in bfloat16 or wider, within the bound.
A program may use at most 128 MiB of HBM per device.

v0:
```python
import jax
import jax.numpy as jnp
from jax import lax
from jax.sharding import PartitionSpec as P

LOSS_SCALE = 8192.0


def extended(shard, sides, width):
    for axis, dim in sides:
        size, length = (lax.axis_size(axis), shard.shape[dim])
        up = [(i, (i + 1) % size) for i in range(size - 1)]
        down = [(j, i) for i, j in up]
        last = lax.slice_in_dim(shard, length - width, length, axis=dim)
        initial = lax.slice_in_dim(shard, 0, width, axis=dim)
        before = lax.ppermute(last, axis, up)
        after = lax.ppermute(initial, axis, down)
        shard = jnp.concatenate([before, shard, after], axis=dim)
    return shard


def shifted(shard, axis, by):
    size = lax.axis_size(axis)
    pairs = [(i, i + by) for i in range(size) if 0 <= i + by < size]
    return lax.ppermute(shard, axis, pairs)


def activate(values):
    return jax.nn.gelu(values, approximate=True)


def activate_slope(values):
    return jax.vjp(activate, values)[1](jnp.ones_like(values))[0]


def patches(field):
    rows_here, cols_here, channels = (field.shape[1], field.shape[2], field.shape[3])
    padded = extended(field, (("fsdp", 1),), 1)
    row_base = lax.axis_index("fsdp") * rows_here % cols_here
    upper = jnp.where(row_base == 0, jnp.zeros_like(padded[:, :1]), padded[:, :1])
    lower = jnp.where(
        row_base + rows_here == cols_here, jnp.zeros_like(padded[:, -1:]), padded[:, -1:]
    )
    padded = jnp.concatenate([upper, padded[:, 1:-1], lower], axis=1)
    padded = jnp.pad(padded, ((0, 0), (0, 0), (1, 1), (0, 0)))
    pieces = [
        padded[:, i : i + rows_here, j : j + cols_here, :] for i in range(3) for j in range(3)
    ]
    return jnp.concatenate(pieces, axis=-1).reshape(-1, 9 * channels)


def contract_rows(left, right):
    return lax.dot_general(
        left, right, (((0,), (0,)), ((), ())), preferred_element_type=jnp.float32
    )


def flipped(kernel):
    channels = kernel.shape[1]
    grid_form = kernel.reshape(3, 3, channels, channels)[::-1, ::-1]
    return jnp.swapaxes(grid_form, 2, 3).reshape(9 * channels, channels)


def section_parts(segment_in, first_conv, second_conv):
    channels = segment_in.shape[-1]
    first_in = activate(segment_in.astype(jnp.float32)).astype(jnp.bfloat16)
    first_patches = patches(first_in)
    hidden = jnp.dot(first_patches, first_conv, preferred_element_type=jnp.float32)
    second_in = activate(hidden).astype(jnp.bfloat16).reshape(segment_in.shape)
    second_patches = patches(second_in)
    update = jnp.dot(second_patches, second_conv, preferred_element_type=jnp.float32)
    output = (segment_in.reshape(-1, channels).astype(jnp.float32) + update).astype(jnp.bfloat16)
    return (output.reshape(segment_in.shape), first_patches, hidden, second_patches)


def section_back(segment_in, out_grad, first_conv, second_conv, first_flip, second_flip):
    channels = segment_in.shape[-1]
    output, first_patches, hidden, second_patches = section_parts(
        segment_in, first_conv, second_conv
    )
    out_rows = out_grad.reshape(-1, channels)
    second_grad = jnp.dot(patches(out_grad), second_flip, preferred_element_type=jnp.float32)
    hidden_grad = (second_grad * activate_slope(hidden)).astype(jnp.bfloat16)
    first_grad = jnp.dot(
        patches(hidden_grad.reshape(segment_in.shape)),
        first_flip,
        preferred_element_type=jnp.float32,
    )
    slope = activate_slope(segment_in.reshape(-1, channels).astype(jnp.float32))
    in_grad = (
        (out_rows.astype(jnp.float32) + first_grad * slope)
        .astype(jnp.bfloat16)
        .reshape(segment_in.shape)
    )
    return (
        in_grad,
        contract_rows(first_patches, hidden_grad),
        contract_rows(second_patches, out_rows),
    )


def head_loss(output, head_weight, tints, targets, factor):
    channels = output.shape[-1]
    out_rows = output.reshape(-1, channels)
    logits = lax.dot_general(
        head_weight, out_rows, (((1,), (1,)), ((), ())), preferred_element_type=jnp.float32
    )
    albedo = jax.nn.sigmoid(logits.reshape(targets.shape))
    tint = jnp.transpose(tints)[:, :, None, None]
    mismatch = albedo * tint - targets
    squares = jnp.sum(mismatch * mismatch)
    logit_grad = (
        (factor * mismatch * tint * albedo * (1.0 - albedo)).astype(jnp.bfloat16).reshape(3, -1)
    )
    head_grad = lax.dot_general(
        logit_grad, out_rows, (((1,), (0,)), ((), ())), preferred_element_type=jnp.float32
    )
    out_grad = lax.dot_general(
        logit_grad, head_weight, (((0,), (0,)), ((), ())), preferred_element_type=jnp.float32
    )
    return (squares, head_grad, out_grad.astype(jnp.bfloat16).reshape(output.shape))


def crop_tints(illum, light_color):
    lights = light_color.shape[0]
    onehot = (illum[..., None] == jnp.arange(lights, dtype=jnp.int32)).astype(jnp.float32)
    return jnp.dot(onehot.reshape(-1, lights), light_color, precision=lax.Precision.HIGHEST)


def crop_targets(photos, offsets, row_base, rows_here, cols_here):

    def one_crop(picture, offset):
        start = (jnp.zeros((), jnp.int32), offset[0] + row_base, offset[1])
        return lax.dynamic_slice(picture, start, (3, rows_here, cols_here))

    cut = jax.vmap(jax.vmap(one_crop))(photos, offsets).astype(jnp.float32)
    return jnp.moveaxis(cut, 2, 0)


def fetch_convs(conv_weight):
    gathered = lax.all_gather(conv_weight[0], "fsdp", axis=1, tiled=True)
    return (gathered[0], gathered[1])


def pass_on(field):
    return shifted(field, "segment", 1)


def pass_back(field):
    return shifted(field, "segment", -1)


def body(hooks, proj_weight, conv_weight, head_weight, light_color, illum, offsets, photos):
    segments = lax.axis_size("segment")
    segment_index = lax.axis_index("segment")
    is_last = segment_index == segments - 1
    micro_count, band_rows, grid_cols, model_width = (
        hooks.shape[1],
        hooks.shape[2],
        hooks.shape[3],
        hooks.shape[4],
    )
    crop_count = 1
    channels = proj_weight.shape[2]
    tokens = hooks[0].reshape(-1, model_width)
    first_global = lax.axis_index("fsdp") * band_rows
    crop_here = first_global // grid_cols
    row_base = first_global % grid_cols
    columns = tokens
    projected = jnp.dot(
        columns,
        lax.all_gather(proj_weight[0], "fsdp", axis=0, tiled=True),
        preferred_element_type=jnp.float32,
    )
    projected = projected.astype(jnp.bfloat16).reshape(
        micro_count, crop_count, band_rows, grid_cols, channels
    )
    first_conv, second_conv = fetch_convs(conv_weight)
    micro_shape = (crop_count, band_rows, grid_cols, channels)
    flat_shape = (micro_count * crop_count, band_rows, grid_cols, channels)
    flat_proj = projected.reshape(flat_shape)
    incoming = jnp.zeros_like(flat_proj)
    for p in range(segments):
        segment_in = (flat_proj.astype(jnp.float32) + incoming.astype(jnp.float32)).astype(
            jnp.bfloat16
        )
        output = section_parts(segment_in, first_conv, second_conv)[0]
        if p + 1 < segments:
            incoming = pass_on(output)
    inputs_all = segment_in.reshape((micro_count,) + micro_shape)
    outputs_all = output.reshape((micro_count,) + micro_shape)
    illum_here = lax.dynamic_slice_in_dim(illum, crop_here, 1, 1)
    offsets_here = lax.dynamic_slice_in_dim(offsets, crop_here, 1, 1)
    photos_here = lax.dynamic_slice_in_dim(photos, crop_here, 1, 1)
    tints = crop_tints(illum_here, light_color)
    targets = crop_targets(photos_here, offsets_here, row_base, band_rows, grid_cols)
    targets = targets.reshape(3, micro_count * crop_count, band_rows, grid_cols)
    npix = 3 * micro_count * lax.axis_size("dp") * band_rows * lax.axis_size("fsdp") * grid_cols
    factor = 2.0 * LOSS_SCALE / npix
    squares, head_grad, out_grads = head_loss(
        outputs_all.reshape(flat_shape), head_weight, tints, targets, factor
    )
    out_grads = out_grads.reshape((micro_count,) + micro_shape)
    back_first, back_second = fetch_convs(conv_weight)
    first_flip = flipped(back_first)
    second_flip = flipped(back_second)
    flat_in = inputs_all.reshape(flat_shape)
    flat_grads = out_grads.reshape(flat_shape)
    received = jnp.zeros_like(flat_grads)
    for p in range(segments):
        out_grad = jnp.where(is_last, flat_grads, received)
        in_grad, first_sum, second_sum = section_back(
            flat_in, out_grad, back_first, back_second, first_flip, second_flip
        )
        if p + 1 < segments:
            received = pass_back(in_grad)
    grad_rows = in_grad.reshape(-1, channels)
    conv_sums = jnp.concatenate([first_sum, second_sum], axis=1)
    columns = tokens
    proj_part = lax.psum_scatter(
        contract_rows(columns, grad_rows), "fsdp", scatter_dimension=0, tiled=True
    )
    conv_part = lax.psum_scatter(conv_sums, "fsdp", scatter_dimension=0, tiled=True)
    proj_part, conv_part = lax.psum((proj_part, conv_part), "dp")
    loss_term = jnp.where(is_last, squares, 0.0)
    head_term = jnp.where(is_last, head_grad, 0.0)
    head_total, square_total = lax.psum((head_term, loss_term), ("segment", "fsdp", "dp"))
    grad_conv = jnp.stack([conv_part[:, :channels], conv_part[:, channels:]])[None]
    return (proj_part[None], grad_conv, head_total, square_total / npix)


def solution(mesh):
    placed = (
        P("segment", "dp", "fsdp", None, None),
        P("segment", "fsdp", None),
        P("segment", None, "fsdp", None),
        P(),
        P(),
        P("dp", None),
        P("dp", None, None),
        P("dp", None, None, None, None),
    )
    return jax.shard_map(
        body,
        mesh=mesh,
        in_specs=placed,
        out_specs=(P("segment", "fsdp", None), P("segment", None, "fsdp", None), P(), P()),
        check_vma=False,
    )
```

profile of v0, /device:TPU:1, one launch (start us, length us, event | category | flops | bytes accessed | tf_op | source)
XLA Modules:
  0.0 882.3 jit_solution(2431889212769604529)
XLA Ops:
  9.6 138.4 %all-gather.5.cloned.1.call-done = bf16[1,6144,256]{2,1,0:T(8,128)(2,1)} async-done(((bf16[1,192,256]{2,1,0:T(8,128)(2,1)}), bf16[1,6144,256]{2,1,0:T(8,128)(2,1)}) %all-gather.5.cloned.1.call-update) | async-done | bytes 3145744 | tf_op jit(solution)/shard_map/all_gather | solution.py:172
  147.9 7.3 fusion.8
  157.1 4.0 collective-permute-start
  171.4 132.0 %all-gather.7.cloned.1.call-done = bf16[1,2,2304,256]{3,2,1,0:T(8,128)(2,1)} async-done(((bf16[1,2,72,256]{3,2,1,0:T(8,128)(2,1)}), bf16[1,2,2304,256]{3,2,1,0:T(8,128)(2,1)}) %all-gather.7.cloned.1.call-update) | async-done | bytes 2359312 | tf_op jit(solution)/shard_map/all_gather | solution.py:141
  303.4 4.2 fusion.54
  312.0 4.4 collective-permute-done.3
  321.9 12.9 %copy.50 = bf16[2,1,3,96,96]{2,1,0,4,3:T(2,128)(2,1)} copy(bf16[2,1,3,96,96]{4,3,2,1,0:T(8,128)(2,1)S(1)} %constant_dynamic-slice_fusion.2) | data formatting | bytes 221184
  334.8 3.3 gather_fusion
  339.5 5.5 collective-permute-done.4
  361.7 3.6 collective-permute-done.8
  375.8 4.1 collective-permute-start.9
  385.2 3.6 collective-permute-start.11
  391.0 3.7 collective-permute-done.12
  397.4 23.5 %collective-permute-start.13 = (bf16[2,8,64,256]{3,2,1,0:T(8,128)(2,1)S(1)}, bf16[2,8,64,256]{3,2,1,0:T(8,128)(2,1)S(1)}, u32[]{:S(2)}, u32[]{:S(2)}) collective-permute-start(bf16[2,8,64,256]{3,2,1,0:T(8,128)(2,1)S(1)} %bitcast.225), channel_id=1, source_target_pairs={{64,0},{65,1},{66,2},{67,3},{68,4},{69,5},{70,6},{71,7},{72,8},{73... | collective-permute-start | bytes 1572872 | tf_op jit(solution)/shard_map/ppermute | solution.py:25
  422.4 4.8 collective-permute-start.14
  430.1 4.8 collective-permute-done.15
  442.2 6.1 copy.48
  448.4 5.8 collective-permute-start.16
  455.7 3.5 collective-permute-done.17
  462.7 16.0 %convolution_bitcast_fusion = f32[6144,256]{0,1:T(8,128)} fusion(bf16[1024,6144]{1,0:T(8,128)(2,1)} %bitcast.223, bf16[1024,256]{1,0:T(8,128)(2,1)S(1)} %bitcast.150, f32[1024,256]{1,0:T(8,128)S(1)} %fusion.36, bf16[1024,2304]{1,0:T(8,128)(2,1)} %copy-done.11, bf16[2304,256]{1,0:T(8,128)(2,1)S(1)} %bitcast.207), kind=kOutput, calls=%fused_computation.1 | convolution fusion | flops 4430233600 | bytes 26345472 | tf_op jit(solution)/shard_map/dot_general | solution.py:53
  478.7 6.6 copy.46
  485.7 119.6 %reduce-scatter.9.cloned.1.call-done = f32[72,512]{1,0:T(8,128)} async-done(((f32[2304,512]{1,0:T(8,128)}), f32[72,512]{1,0:T(8,128)}) %reduce-scatter.9.cloned.1.call-update) | async-done | bytes 147472
  607.1 171.1 %reduce-scatter.7.cloned.1.call-done = f32[192,256]{1,0:T(8,128)} async-done(((f32[6144,256]{1,0:T(8,128)}), f32[192,256]{1,0:T(8,128)}) %reduce-scatter.7.cloned.1.call-update) | async-done | bytes 196624
  782.0 88.2 %all-reduce.8 = (f32[3,256]{1,0:T(4,128)}, f32[]{:T(128)}) all-reduce(f32[3,256]{1,0:T(4,128)S(1)} %convolution_select_fusion, f32[]{:T(128)S(6)} %select_n.191), channel_id=1, replica_groups=mesh['segment'=2,'fsdp'=32,'dp'=2] {'segment','fsdp','dp'}, use_global_device_ids=true, to_apply=%region_4.5 | all-reduce | flops 769 | bytes 6152 | tf_op jit(solution)/shard_map/psum | solution.py:227
  (248 shorter events, 87.8 us)
Async XLA Ops:
  7.2 140.8 %all-gather.5.cloned.1.call-start = ((), (), s32[]{:S(2)}) async-start(), calls=%async_computation.2 | async-start | bytes 3244032 | tf_op jit(solution)/shard_map/all_gather | solution.py:172
  7.9 295.4 %all-gather.7.cloned.1.call-start = ((), (), s32[]{:S(2)}) async-start(), calls=%async_computation.3 | async-start | bytes 2433024 | tf_op jit(solution)/shard_map/all_gather | solution.py:141
  8.7 596.7 %reduce-scatter.9.cloned.1.call-start = ((), (), s32[]{:S(2)}) async-start(), calls=%async_computation.5 | async-start | bytes 4866048
  155.6 5.4 collective-permute-start.1
  157.1 5.3 collective-permute-start
  307.6 4.4 collective-permute-start.2
  310.6 5.7 collective-permute-start.3
  320.4 24.6 %collective-permute-start.4 = (bf16[2,8,64,256]{3,2,1,0:T(8,128)(2,1)S(1)}, bf16[2,8,64,256]{3,2,1,0:T(8,128)(2,1)S(1)}, u32[]{:S(2)}, u32[]{:S(2)}) collective-permute-start(bf16[2,8,64,256]{3,2,1,0:T(8,128)(2,1)S(1)} %bitcast.224), channel_id=1, source_target_pairs={{0,64},{1,65},{2,66},{3,67},{4,68},{5,69},{6,70},{7,71},{8,72},{9,... | collective-permute-start | bytes 1572872 | tf_op jit(solution)/shard_map/ppermute | solution.py:25
  345.4 5.2 collective-permute-start.5
  348.9 5.0 collective-permute-start.6
  358.4 3.3 collective-permute-start.7
  360.3 5.0 collective-permute-start.8
  372.1 7.7 collective-permute-start.10
  375.8 5.7 collective-permute-start.9
  385.2 5.7 collective-permute-start.11
  389.5 5.2 collective-permute-start.12
  397.4 25.0 %collective-permute-start.13 = (bf16[2,8,64,256]{3,2,1,0:T(8,128)(2,1)S(1)}, bf16[2,8,64,256]{3,2,1,0:T(8,128)(2,1)S(1)}, u32[]{:S(2)}, u32[]{:S(2)}) collective-permute-start(bf16[2,8,64,256]{3,2,1,0:T(8,128)(2,1)S(1)} %bitcast.225), channel_id=1, source_target_pairs={{64,0},{65,1},{66,2},{67,3},{68,4},{69,5},{70,6},{71,7},{72,8},{73... | collective-permute-start | bytes 1572872 | tf_op jit(solution)/shard_map/ppermute | solution.py:25
  422.4 7.7 collective-permute-start.14
  427.3 7.6 collective-permute-start.15
  448.3 329.9 %reduce-scatter.7.cloned.1.call-start = ((), (), s32[]{:S(2)}) async-start(), calls=%async_computation.4 | async-start | bytes 6488064
  448.4 7.3 collective-permute-start.16
  454.1 5.0 collective-permute-start.17
  485.3 389.2 %copy-start.1 = (bf16[2,4,3,96,96]{4,3,2,1,0:T(8,128)(2,1)S(1)}, bf16[2,4,3,96,96]{4,3,2,1,0:T(8,128)(2,1)}, u32[]{:S(2)}) copy-start(bf16[2,4,3,96,96]{4,3,2,1,0:T(8,128)(2,1)} %param.15) | copy-start | bytes 1327108
  485.3 385.6 %all-reduce.12.cloned.1.call-start = ((), (), s32[]{:S(2)}) async-start(), calls=%async_computation.6 | async-start | bytes 1048576 | tf_op jit(solution)/shard_map/psum | solution.py:224
  (21 other events, 1053.9 us)
Sparse Core Ops, SparseCore 0:
  9.7 138.2 all-gather.4
  149.6 153.7 all-gather.6
  448.4 156.8 reduce-scatter.8
  607.6 170.5 reduce-scatter.6
  780.5 55.5 all-reduce.11
where the time goes:
time: 890 us; the launch traced here: 882 us
  waiting for transfers between devices  595 us (67%)
  blocking collectives  88.2 us (10%)
  starting transfers between devices  65 us (7%)
  local copies, waits for them, and re-layouts  62.2 us (7%)
  matrix products  41.6 us (5%)
  between operations  17.8 us (2%)
  other arithmetic  12.8 us (1%)
    unnamed x7, waiting for transfers between devices  292 us
    all_gather x1, waiting for transfers between devices, body(): lax.all_gather(proj_weight[0], 'fsdp', axis=0, tiled=True)  138 us
    all_gather x1, waiting for transfers between devices, fetch_convs(): gathered = lax.all_gather(conv_weight[0], 'fsdp', axis=1, tiled=True)  132 us
    psum x1, blocking collectives, body(): lax.psum((head_term, loss_term), ('segment', 'fsdp', 'dp'))  88.2 us
    unnamed x114, local copies, waits for them, and re-layouts  46.8 us
    ppermute x8, starting transfers between devices, extended(): before = lax.ppermute(last, axis, up)  28.8 us
    ppermute x2, starting transfers between devices, shifted(): return lax.ppermute(shard, axis, pairs)  24.7 us
    ppermute x8, waiting for transfers between devices, extended(): after = lax.ppermute(initial, axis, down)  23.1 us
  transfers between devices with their start and end apart: 23, of which 14 were waited for; matrix products, arithmetic and copies ran while one was open for 8% of the time, Pallas kernels for 0%

commit v1 on v0

--- a/solution.py
+++ b/solution.py
@@ -224,7 +224,7 @@
     proj_part, conv_part = lax.psum((proj_part, conv_part), "dp")
     loss_term = jnp.where(is_last, squares, 0.0)
     head_term = jnp.where(is_last, head_grad, 0.0)
-    head_total, square_total = lax.psum((head_term, loss_term), ("segment", "fsdp", "dp"))
+    head_total, square_total = lax.psum(lax.psum((head_term, loss_term), ("fsdp", "dp")), "segment")
     grad_conv = jnp.stack([conv_part[:, :channels], conv_part[:, channels:]])[None]
     return (proj_part[None], grad_conv, head_total, square_total / npix)
 

time: 890 us -> 1010 us (1.13)
  blocking collectives: 88.2 us -> 204 us
    psum x1 -> x2, blocking collectives: 88.2 us -> 204 us  [the longest x1 151 us: body(): lax.psum((head_term, loss_term), ('fsdp', 'dp'))]
  transfers between devices with their start and end apart: 23 -> 23, of which waited for: 14 -> 14; matrix products, arithmetic and copies ran while one was open for 8% -> 7% of each run, Pallas kernels for 0% -> 0%
where the time goes in v1:
time: 1010 us; the launch traced here: 998 us
  waiting for transfers between devices  595 us (59%)
  blocking collectives  204 us (20%)
  starting transfers between devices  65 us (6%)
  local copies, waits for them, and re-layouts  62.2 us (6%)
  matrix products  41.6 us (4%)
  between operations  17.8 us (2%)
  other arithmetic  12.8 us (1%)
    unnamed x7, waiting for transfers between devices  292 us
    psum x1, blocking collectives, body(): lax.psum((head_term, loss_term), ('fsdp', 'dp'))  151 us
    all_gather x1, waiting for transfers between devices, body(): lax.all_gather(proj_weight[0], 'fsdp', axis=0, tiled=True)  138 us
    all_gather x1, waiting for transfers between devices, fetch_convs(): gathered = lax.all_gather(conv_weight[0], 'fsdp', axis=1, tiled=True)  132 us
    psum x1, blocking collectives, body(): lax.psum(lax.psum((head_term, loss_term), ('fsdp', 'dp')), 'segment')  53.5 us
    unnamed x114, local copies, waits for them, and re-layouts  46.9 us
    ppermute x8, starting transfers between devices, extended(): before = lax.ppermute(last, axis, up)  28.9 us
    ppermute x2, starting transfers between devices, shifted(): return lax.ppermute(shard, axis, pairs)  24.7 us
  transfers between devices with their start and end apart: 23, of which 14 were waited for; matrix products, arithmetic and copies ran while one was open for 7% of the time, Pallas kernels for 0%

profile of v1, /device:TPU:1, one launch (start us, length us, event | category | flops | bytes accessed | tf_op | source)
XLA Modules:
  0.0 998.1 jit_solution(16181815280689369281)
XLA Ops:
  9.6 138.4 %all-gather.5.cloned.1.call-done = bf16[1,6144,256]{2,1,0:T(8,128)(2,1)} async-done(((bf16[1,192,256]{2,1,0:T(8,128)(2,1)}), bf16[1,6144,256]{2,1,0:T(8,128)(2,1)}) %all-gather.5.cloned.1.call-update) | async-done | bytes 3145744 | tf_op jit(solution)/shard_map/all_gather | solution.py:172
  147.9 7.3 fusion.8
  157.1 4.0 collective-permute-start
  171.4 132.0 %all-gather.7.cloned.1.call-done = bf16[1,2,2304,256]{3,2,1,0:T(8,128)(2,1)} async-done(((bf16[1,2,72,256]{3,2,1,0:T(8,128)(2,1)}), bf16[1,2,2304,256]{3,2,1,0:T(8,128)(2,1)}) %all-gather.7.cloned.1.call-update) | async-done | bytes 2359312 | tf_op jit(solution)/shard_map/all_gather | solution.py:141
  303.4 4.2 fusion.54
  312.0 4.4 collective-permute-done.3
  321.9 12.9 %copy.50 = bf16[2,1,3,96,96]{2,1,0,4,3:T(2,128)(2,1)} copy(bf16[2,1,3,96,96]{4,3,2,1,0:T(8,128)(2,1)S(1)} %constant_dynamic-slice_fusion.2) | data formatting | bytes 221184
  339.4 5.6 collective-permute-done.4
  361.7 3.6 collective-permute-done.8
  375.8 4.1 collective-permute-start.9
  385.3 3.6 collective-permute-start.11
  391.0 3.7 collective-permute-done.12
  397.4 23.5 %collective-permute-start.13 = (bf16[2,8,64,256]{3,2,1,0:T(8,128)(2,1)S(1)}, bf16[2,8,64,256]{3,2,1,0:T(8,128)(2,1)S(1)}, u32[]{:S(2)}, u32[]{:S(2)}) collective-permute-start(bf16[2,8,64,256]{3,2,1,0:T(8,128)(2,1)S(1)} %bitcast.225), channel_id=1, source_target_pairs={{64,0},{65,1},{66,2},{67,3},{68,4},{69,5},{70,6},{71,7},{72,8},{73... | collective-permute-start | bytes 1572872 | tf_op jit(solution)/shard_map/ppermute | solution.py:25
  422.5 4.9 collective-permute-start.14
  430.2 4.8 collective-permute-done.15
  442.3 6.1 copy.48
  448.5 5.7 collective-permute-start.16
  455.8 3.5 collective-permute-done.17
  462.8 15.9 %convolution_bitcast_fusion = f32[6144,256]{0,1:T(8,128)} fusion(bf16[1024,6144]{1,0:T(8,128)(2,1)} %bitcast.223, bf16[1024,256]{1,0:T(8,128)(2,1)S(1)} %bitcast.150, f32[1024,256]{1,0:T(8,128)S(1)} %fusion.36, bf16[1024,2304]{1,0:T(8,128)(2,1)} %copy-done.11, bf16[2304,256]{1,0:T(8,128)(2,1)S(1)} %bitcast.207), kind=kOutput, calls=%fused_computation.1 | convolution fusion | flops 4430233600 | bytes 26345472 | tf_op jit(solution)/shard_map/dot_general | solution.py:53
  478.7 6.6 copy.46
  485.8 119.2 %reduce-scatter.9.cloned.1.call-done = f32[72,512]{1,0:T(8,128)} async-done(((f32[2304,512]{1,0:T(8,128)}), f32[72,512]{1,0:T(8,128)}) %reduce-scatter.9.cloned.1.call-update) | async-done | bytes 147472
  606.8 171.3 %reduce-scatter.7.cloned.1.call-done = f32[192,256]{1,0:T(8,128)} async-done(((f32[6144,256]{1,0:T(8,128)}), f32[192,256]{1,0:T(8,128)}) %reduce-scatter.7.cloned.1.call-update) | async-done | bytes 196624
  781.9 150.6 %all-reduce.8 = (f32[3,256]{1,0:T(4,128)S(1)}, f32[]{:T(128)}) all-reduce(f32[3,256]{1,0:T(4,128)S(1)} %convolution_select_fusion, f32[]{:T(128)S(6)} %select_n.191), channel_id=1, replica_groups=mesh['segment'=2,'fsdp'=32,'dp'=2] {'fsdp','dp'}, use_global_device_ids=true, to_apply=%region_4.5 | all-reduce | flops 769 | bytes 6152 | tf_op jit(solution)/shard_map/psum | solution.py:227
  932.5 53.5 %all-reduce.10 = (f32[3,256]{1,0:T(4,128)}, f32[]{:T(128)}) all-reduce(f32[3,256]{1,0:T(4,128)S(1)} %get-tuple-element.20, f32[]{:T(128)} %get-tuple-element.21), channel_id=1, replica_groups=mesh['segment'=2,'fsdp'=32,'dp'=2] {'segment'}, use_global_device_ids=true, to_apply=%region_5.6 | all-reduce | flops 769 | bytes 6152 | tf_op jit(solution)/shard_map/psum | solution.py:227
  (249 shorter events, 91.0 us)
Async XLA Ops:
  7.2 140.8 %all-gather.5.cloned.1.call-start = ((), (), s32[]{:S(2)}) async-start(), calls=%async_computation.2 | async-start | bytes 3244032 | tf_op jit(solution)/shard_map/all_gather | solution.py:172
  7.9 295.4 %all-gather.7.cloned.1.call-start = ((), (), s32[]{:S(2)}) async-start(), calls=%async_computation.3 | async-start | bytes 2433024 | tf_op jit(solution)/shard_map/all_gather | solution.py:141
  8.7 596.4 %reduce-scatter.9.cloned.1.call-start = ((), (), s32[]{:S(2)}) async-start(), calls=%async_computation.5 | async-start | bytes 4866048
  155.6 5.4 collective-permute-start.1
  157.1 5.3 collective-permute-start
  307.6 4.4 collective-permute-start.2
  310.6 5.7 collective-permute-start.3
  320.4 24.6 %collective-permute-start.4 = (bf16[2,8,64,256]{3,2,1,0:T(8,128)(2,1)S(1)}, bf16[2,8,64,256]{3,2,1,0:T(8,128)(2,1)S(1)}, u32[]{:S(2)}, u32[]{:S(2)}) collective-permute-start(bf16[2,8,64,256]{3,2,1,0:T(8,128)(2,1)S(1)} %bitcast.224), channel_id=1, source_target_pairs={{0,64},{1,65},{2,66},{3,67},{4,68},{5,69},{6,70},{7,71},{8,72},{9,... | collective-permute-start | bytes 1572872 | tf_op jit(solution)/shard_map/ppermute | solution.py:25
  345.4 5.2 collective-permute-start.5
  348.9 5.0 collective-permute-start.6
  358.4 3.3 collective-permute-start.7
  360.3 5.0 collective-permute-start.8
  372.2 7.7 collective-permute-start.10
  375.8 5.7 collective-permute-start.9
  385.3 5.7 collective-permute-start.11
  389.5 5.2 collective-permute-start.12
  397.4 25.0 %collective-permute-start.13 = (bf16[2,8,64,256]{3,2,1,0:T(8,128)(2,1)S(1)}, bf16[2,8,64,256]{3,2,1,0:T(8,128)(2,1)S(1)}, u32[]{:S(2)}, u32[]{:S(2)}) collective-permute-start(bf16[2,8,64,256]{3,2,1,0:T(8,128)(2,1)S(1)} %bitcast.225), channel_id=1, source_target_pairs={{64,0},{65,1},{66,2},{67,3},{68,4},{69,5},{70,6},{71,7},{72,8},{73... | collective-permute-start | bytes 1572872 | tf_op jit(solution)/shard_map/ppermute | solution.py:25
  422.5 7.7 collective-permute-start.14
  427.4 7.6 collective-permute-start.15
  448.4 329.7 %reduce-scatter.7.cloned.1.call-start = ((), (), s32[]{:S(2)}) async-start(), calls=%async_computation.4 | async-start | bytes 6488064
  448.5 7.3 collective-permute-start.16
  454.2 5.0 collective-permute-start.17
  485.3 504.9 %copy-start.1 = (bf16[2,4,3,96,96]{4,3,2,1,0:T(8,128)(2,1)S(1)}, bf16[2,4,3,96,96]{4,3,2,1,0:T(8,128)(2,1)}, u32[]{:S(2)}) copy-start(bf16[2,4,3,96,96]{4,3,2,1,0:T(8,128)(2,1)} %param.15) | copy-start | bytes 1327108
  485.4 501.3 %all-reduce.13.cloned.1.call-start = ((), (), s32[]{:S(2)}) async-start(), calls=%async_computation.6 | async-start | bytes 1048576 | tf_op jit(solution)/shard_map/psum | solution.py:224
  (21 other events, 1053.7 us)
Sparse Core Ops, SparseCore 0:
  9.7 138.2 all-gather.4
  149.6 153.7 all-gather.6
  448.5 156.4 reduce-scatter.8
  607.3 170.7 reduce-scatter.6
  780.4 56.8 all-reduce.12
